TPU v7x, 32 devices: a whole 2x2x4 slice. The times are simulated.
32 devices in a mesh: section: 2 (over y), batch: 16 (over z, x, core).
Axes of the slice: x: 2, y: 2, z: 4, core: 2. Of those that a mesh axis runs over, the one named last changes fastest.
Arguments:
- images: bfloat16 [32, 64, 3072], P('batch', None, 'section'), may hold values from -1 to 1
- noise_draw: bfloat16 [32, 64, 3072], P('batch', None, 'section'), may hold values from -6 to 6
- cotangent: bfloat16 [32, 64, 3072], P('batch', None, 'section'), may hold values from -6 to 6
- hue_angle: float32 [32], P('batch'), may hold values from -0.5 to 0.5
- saturation: float32 [32], P('batch'), may hold values from 0.5 to 1.5
- timestep: int32 [32], P('batch'), may hold values from 50 to 199
- stem_weight: bfloat16 [3072, 1024], P('section'), may hold values from -0.109375 to 0.109375
- conv_weight: bfloat16 [2, 9216, 1024], P('section', 'batch'), may hold values from -0.0625 to 0.0625
- emb_weight: bfloat16 [2, 1024, 2048], P('section'), may hold values from -0.1875 to 0.1875
- head_weight: bfloat16 [1024, 3072], P(None, 'section'), may hold values from -0.1875 to 0.1875
Outputs:
- purified: bfloat16 [32, 64, 3072], P('batch', None, 'section')
- colour_grad: float32 [32, 2], P('batch')
All inputs are finite; a program needn't handle non-finite values.
Results may differ from a plain program's by a relative error of at most 0.039.
Values may be sent and summed in bfloat16 or wider, within the bound.
A program may use at most 128 MiB of HBM per device.

v0:
```python
import math
import jax
import jax.numpy as jnp
from jax import lax
from jax.sharding import PartitionSpec as P

CH = 1024
GROUPS = 32
TEMB = 1024
GRID = 8
TSTEPS = 1000
PV = 3072


def shifted(value, axis, steps):
    count = lax.axis_size(axis)
    pairs = [(source, (source + steps) % count) for source in range(count)]
    return lax.ppermute(value, axis, pairs)


def from_root(block, axis, holder):
    block = jnp.where(lax.axis_index(axis) == holder, block, jnp.zeros_like(block))
    return lax.psum(block, axis)


def noise_levels(timestep):
    beta_rates = jnp.linspace(0.0001, 0.02, TSTEPS, dtype=jnp.float32)
    levels = jnp.cumprod(1.0 - beta_rates)
    chosen = jnp.arange(TSTEPS, dtype=jnp.int32)[None, :] == timestep[:, None]
    return jnp.sum(jnp.where(chosen, levels[None, :], jnp.float32(0.0)), axis=1)


def time_features(timestep):
    half_width = TEMB // 2
    frequency = jnp.exp(-math.log(10000.0) * jnp.arange(half_width, dtype=jnp.float32) / half_width)
    angles = timestep.astype(jnp.float32)[:, None] * frequency[None, :]
    return jax.nn.silu(jnp.concatenate([jnp.cos(angles), jnp.sin(angles)], axis=1)).astype(
        jnp.bfloat16
    )


def colour_maps(hue_angle, saturation):
    grey_map = jnp.full((3, 3), 1.0 / 3.0, dtype=jnp.float32)
    rotate_map = jnp.eye(3, dtype=jnp.float32) - grey_map
    cross_map = jnp.array(
        [[0.0, -1.0, 1.0], [1.0, 0.0, -1.0], [-1.0, 1.0, 0.0]], dtype=jnp.float32
    ) / math.sqrt(3.0)
    cosine = jnp.cos(hue_angle)[:, None, None]
    sine_of = jnp.sin(hue_angle)[:, None, None]
    turning = cosine * rotate_map + sine_of * cross_map
    sat_scale = saturation[:, None, None]
    matrix = grey_map + sat_scale * turning
    hue_slope = sat_scale * (cosine * cross_map - sine_of * rotate_map)
    return (matrix, hue_slope, turning)


def apply_map(matrix, pixels):
    return jnp.sum(matrix[:, None, None, :, :] * pixels[:, :, :, None, :], axis=-1)


def conv_branch(feature, weight, scaling):
    number = feature.shape[0]
    channels = feature.shape[2]
    grouped = feature.reshape(number, GRID * GRID, GROUPS, channels // GROUPS)
    centre = jnp.mean(grouped, axis=(1, 3), keepdims=True)
    spread_sq = jnp.mean(jnp.square(grouped - centre), axis=(1, 3), keepdims=True)
    normed = ((grouped - centre) * lax.rsqrt(spread_sq + 1e-05)).reshape(
        number, GRID * GRID, channels
    )
    factor = scaling[:, None, :channels]
    offset = scaling[:, None, channels:]
    active = jax.nn.silu(normed * (1.0 + factor) + offset).astype(jnp.bfloat16)
    padded = jnp.pad(active.reshape(number, GRID, GRID, channels), ((0, 0), (1, 1), (1, 1), (0, 0)))
    taps = [
        padded[:, row_tap : row_tap + GRID, col_tap : col_tap + GRID, :]
        for row_tap in range(3)
        for col_tap in range(3)
    ]
    columns = jnp.concatenate(taps, axis=-1).reshape(number * GRID * GRID, 9 * channels)
    product = jnp.dot(columns, weight, preferred_element_type=jnp.float32)
    return product.reshape(number, GRID * GRID, channels)


def residual_block(feature, weight, scaling):
    primal = feature.astype(jnp.float32)
    return (primal + conv_branch(primal, weight, scaling)).astype(jnp.bfloat16)


def block_adjoint(feature, weight, scaling, upstream):
    primal = feature.astype(jnp.float32)

    def branch_only(probe):
        return conv_branch(probe, weight, scaling)

    _, pullback = jax.vjp(branch_only, primal)
    upstream_f = upstream.astype(jnp.float32)
    return (upstream_f + pullback(upstream_f)[0]).astype(jnp.bfloat16)


def section_total(partial_sum):
    return lax.psum(partial_sum.astype(jnp.bfloat16), "section").astype(jnp.float32)


def send_forward(value):
    return shifted(value, "section", 1)


def send_backward(value):
    return shifted(value, "section", -1)


def spread(value, owner):
    return from_root(value, "section", owner)


def store_one(buffer, value, index_at, is_live):
    previous = lax.dynamic_index_in_dim(buffer, index_at, 0, keepdims=False)
    return lax.dynamic_update_index_in_dim(buffer, jnp.where(is_live, value, previous), index_at, 0)


def run_chain(position, entering, worker, sender):
    number = entering.shape[0]
    clocks = number + lax.axis_size("section") - 1

    def advance(clock, state_in):
        incoming, sources, results = state_in
        member = clock - position
        is_live = (member >= 0) & (member < number)
        index_at = jnp.clip(member, 0, number - 1)
        entry_row = lax.dynamic_index_in_dim(entering, index_at, 0, keepdims=False)
        source = jnp.where(position == 0, entry_row, incoming)

        def run_work():
            return worker(source, index_at)

        def pass_through():
            return source

        result = lax.cond(is_live, run_work, pass_through)
        sources = store_one(sources, source, index_at, is_live)
        results = store_one(results, result, index_at, is_live)
        return (sender(result), sources, results)

    start = (jnp.zeros_like(entering[0]), jnp.zeros_like(entering), jnp.zeros_like(entering))
    final_state = lax.fori_loop(0, clocks, advance, start)
    return (final_state[1], final_state[2])


def local(
    images,
    noise_draw,
    cotangent,
    hue_angle,
    saturation,
    timestep,
    stem_weight,
    conv_weight,
    emb_weight,
    head_weight,
):
    sections = lax.axis_size("section")
    place = lax.axis_index("section")
    number = images.shape[0]
    columns_here = images.shape[2]
    full_conv = lax.all_gather(conv_weight, "batch", axis=1, tiled=True)[0]
    level = noise_levels(timestep)
    root_level = jnp.sqrt(level)[:, None, None]
    root_noise = jnp.sqrt(1.0 - level)[:, None, None]
    matrix, hue_slope, sat_slope = colour_maps(hue_angle, saturation)
    pixels = images.astype(jnp.float32).reshape(number, GRID * GRID, columns_here // 3, 3)
    coloured = apply_map(matrix, pixels).reshape(number, GRID * GRID, columns_here)
    noised = root_level * coloured + root_noise * noise_draw.astype(jnp.float32)
    entry_part = jnp.dot(
        noised.astype(jnp.bfloat16).reshape(-1, columns_here),
        stem_weight,
        preferred_element_type=jnp.float32,
    )
    first = section_total(entry_part).astype(jnp.bfloat16).reshape(number, GRID * GRID, CH)
    offsets = jnp.dot(time_features(timestep), emb_weight[0], preferred_element_type=jnp.float32)

    def forward_work(source, index_at):
        scaling = lax.dynamic_slice_in_dim(offsets, index_at, 1, 0)
        return residual_block(source[None], full_conv, scaling)[0]

    fwd_inputs, fwd_outputs = run_chain(place, first, forward_work, send_forward)
    finals = spread(fwd_outputs, sections - 1)
    predicted = jnp.dot(finals.reshape(-1, CH), head_weight, preferred_element_type=jnp.float32)
    predicted = predicted.reshape(number, GRID * GRID, columns_here)
    purified = ((noised - root_noise * predicted) / root_level).astype(jnp.bfloat16)
    weighted = cotangent.astype(jnp.float32) * (1.0 / math.sqrt(GRID * GRID * PV))
    eps_grad = (-(root_noise / root_level) * weighted).astype(jnp.bfloat16)
    seed_part = lax.dot_general(
        eps_grad.reshape(-1, columns_here),
        head_weight,
        (((1,), (1,)), ((), ())),
        preferred_element_type=jnp.float32,
    )
    seed = section_total(seed_part).astype(jnp.bfloat16).reshape(number, GRID * GRID, CH)

    def adjoint_work(source, index_at):
        saved = lax.dynamic_index_in_dim(fwd_inputs, index_at, 0, keepdims=True)
        scaling = lax.dynamic_slice_in_dim(offsets, index_at, 1, 0)
        return block_adjoint(saved, full_conv, scaling, source[None])[0]

    back_inputs, back_outputs = run_chain(sections - 1 - place, seed, adjoint_work, send_backward)
    grads = spread(back_outputs, 0)
    stem_back = lax.dot_general(
        grads.reshape(-1, CH),
        stem_weight,
        (((1,), (1,)), ((), ())),
        preferred_element_type=jnp.float32,
    )
    stem_back = stem_back.reshape(number, GRID * GRID, columns_here)
    pixel_grad = (weighted + root_level * stem_back).reshape(
        number, GRID * GRID, columns_here // 3, 3
    )
    hue_part = jnp.sum(pixel_grad * apply_map(hue_slope, pixels), axis=(1, 2, 3))
    sat_part = jnp.sum(pixel_grad * apply_map(sat_slope, pixels), axis=(1, 2, 3))
    colour_grad = section_total(jnp.stack([hue_part, sat_part], axis=1))
    return (purified, colour_grad)


def solution(mesh):
    in_specs = (
        P("batch", None, "section"),
        P("batch", None, "section"),
        P("batch", None, "section"),
        P("batch"),
        P("batch"),
        P("batch"),
        P("section", None),
        P("section", "batch", None),
        P("section", None, None),
        P(None, "section"),
    )
    out_specs = (P("batch", None, "section"), P("batch", None))
    return jax.shard_map(local, mesh=mesh, in_specs=in_specs, out_specs=out_specs, check_vma=False)
```

profile of v0, /device:TPU:0, one launch (start us, length us, event | category | flops | bytes accessed | tf_op | source)
XLA Modules:
  0.0 400.9 jit_solution(12375936215744181771)
XLA Ops:
  8.9 3.1 copy.20
  12.0 3.4 copy.21
  15.4 3.4 multiply_reduce_fusion.2
  18.9 3.3 copy.22
  22.2 3.4 copy.23
  26.4 1.6 fusion.82
  28.1 3.2 convolution_convert_fusion.2
  31.3 1.9 convolution_convert_fusion.1
  34.0 3.4 fusion.58
  37.4 27.4 %all-reduce.18.cloned.1.call-done = (bf16[2,64,1024]{2,1,0:T(8,128)(2,1)}, bf16[2,64,1024]{2,1,0:T(8,128)(2,1)}) async-done(((bf16[2,64,1024]{2,1,0:T(8,128)(2,1)}, bf16[2,64,1024]{2,1,0:T(8,128)(2,1)}), (bf16[2,64,1024]{2,1,0:T(8,128)(2,1)}, bf16[2,64,1024]{2,1,0:T(8,128)(2,1)})) %all-reduce.18.cloned.1.call-update) | async-done | bytes 524304 | tf_op jit(solution)/shard_map/psum | solution.py:101
  64.8 72.1 %all-gather.2.cloned.1.call-done = bf16[1,9216,1024]{2,1,0:T(8,128)(2,1)} async-done(((bf16[1,576,1024]{2,1,0:T(8,128)(2,1)}), bf16[1,9216,1024]{2,1,0:T(8,128)(2,1)}) %all-gather.2.cloned.1.call-update) | async-done | bytes 18874384 | tf_op jit(solution)/shard_map/all_gather | solution.py:165
  138.3 72.6 %while.34 = (s32[]{:T(128)}, bf16[64,1024]{1,0:T(8,128)(2,1)}, bf16[2,64,1024]{2,1,0:T(8,128)(2,1)S(1)}, bf16[2,64,1024]{2,1,0:T(8,128)(2,1)}, s32[]{:T(128)}, /...) while((s32[]{:T(128)}, bf16[64,1024]{1,0:T(8,128)(2,1)}, ...), condition=%wide.region_12.13_spmd, body=%wide.region_5.12_spmd.sunk | while | flops 1210057728 | bytes 25409360 | solution.py:145
  138.3 1.0 bitcast_dynamic-update-slice_fusion.6
  139.3 18.3 %conditional.4 = (bf16[64,1024]{1,0:T(8,128)(2,1)S(1)}) conditional(s32[]{:T(128)} %convert_element_type.245, bf16[64,1024]{1,0:T(8,128)(2,1)S(1)} %get-tuple-element.587, (bf16[64,1024]{1,0:T(8,128)(2,1)S(1)}, s32[]{:T(128)}, f32[2,2048]{1,0:T(2,128)}, bf16[9216,1024]{1,0:T(8,128)(2,1)}) %tuple.116), branch_computations={%region_6.6_spmd, %region_7.11_spmd} | conditional | flops 1209861120 | bytes 23311430 | solution.py:139
  147.8 9.8 %fusion = bf16[64,1024]{1,0:T(8,128)(2,1)S(1)} fusion(bf16[64,9216]{1,0:T(8,128)(2,1)S(1)} %fusion.32, bf16[9216,1024]{1,0:T(8,128)(2,1)} %get-tuple-element.369, bf16[64,1024]{1,0:T(8,128)(2,1)S(1)} %get-tuple-element.366), kind=kOutput, calls=%fused_computation.1 | convolution fusion | flops 1208156160 | bytes 20316160 | tf_op jit(solution)/shard_map/while/body/eval_jaxpr/cond/branch_1_fun/dot_general | solution.py:80
  157.7 0.9 constant_dynamic-slice_fusion.7
  159.3 4.1 %collective-permute-done = bf16[64,1024]{1,0:T(8,128)(2,1)} collective-permute-done((bf16[64,1024]{1,0:T(8,128)(2,1)S(1)}, bf16[64,1024]{1,0:T(8,128)(2,1)}, u32[]{:S(2)}, u32[]{:S(2)}) %collective-permute-start) | collective-permute-done | bytes 131104 | tf_op jit(solution)/shard_map/while/body/eval_jaxpr/ppermute | solution.py:18
  163.5 1.0 bitcast_dynamic-update-slice_fusion.6
  164.5 18.3 %conditional.4 = (bf16[64,1024]{1,0:T(8,128)(2,1)S(1)}) conditional(s32[]{:T(128)} %convert_element_type.245, bf16[64,1024]{1,0:T(8,128)(2,1)S(1)} %get-tuple-element.587, (bf16[64,1024]{1,0:T(8,128)(2,1)S(1)}, s32[]{:T(128)}, f32[2,2048]{1,0:T(2,128)}, bf16[9216,1024]{1,0:T(8,128)(2,1)}) %tuple.116), branch_computations={%region_6.6_spmd, %region_7.11_spmd} | conditional | flops 1209861120 | bytes 23311430 | solution.py:139
  172.9 9.8 %fusion = bf16[64,1024]{1,0:T(8,128)(2,1)S(1)} fusion(bf16[64,9216]{1,0:T(8,128)(2,1)S(1)} %fusion.32, bf16[9216,1024]{1,0:T(8,128)(2,1)} %get-tuple-element.369, bf16[64,1024]{1,0:T(8,128)(2,1)S(1)} %get-tuple-element.366), kind=kOutput, calls=%fused_computation.1 | convolution fusion | flops 1208156160 | bytes 20316160 | tf_op jit(solution)/shard_map/while/body/eval_jaxpr/cond/branch_1_fun/dot_general | solution.py:80
  183.2 0.9 constant_dynamic-slice_fusion.7
  184.8 3.1 collective-permute-done
  187.9 1.0 bitcast_dynamic-update-slice_fusion.6
  188.9 19.0 %collective-permute-start = (bf16[64,1024]{1,0:T(8,128)(2,1)S(1)}, bf16[64,1024]{1,0:T(8,128)(2,1)}, u32[]{:S(2)}, u32[]{:S(2)}) collective-permute-start(bf16[64,1024]{1,0:T(8,128)(2,1)S(1)} %get-tuple-element.674), channel_id=1, source_target_pairs={{0,16},{16,0},{1,17},{17,1},{2,18},{18,2},{3,19},{19,3},{4,20},{20... | collective-permute-start | bytes 393224 | tf_op jit(solution)/shard_map/while/body/eval_jaxpr/ppermute | solution.py:18
  207.9 0.9 constant_dynamic-slice_fusion.7
  209.5 1.5 collective-permute-done
  212.3 138.6 %while.35 = (s32[]{:T(128)}, bf16[64,1024]{1,0:T(8,128)(2,1)}, bf16[2,64,1024]{2,1,0:T(8,128)(2,1)}, s32[]{:T(128)}, pred[]{:T(512)}, /*index=5*/bf16[2,64,1024]...) while((s32[]{:T(128)}, bf16[64,1024]{1,0:T(8,128)(2,1)}, ...), condition=%wide.region_28.29_spmd, body=%wide.region_15.28_spmd.sunk | while | flops 1212769664 | bytes 27270924 | solution.py:145
  212.3 1.0 bitcast_select_fusion.7
  213.3 42.1 %collective-permute-start.1 = (bf16[64,1024]{1,0:T(8,128)(2,1)S(1)}, bf16[64,1024]{1,0:T(8,128)(2,1)}, u32[]{:S(2)}, u32[]{:S(2)}) collective-permute-start(bf16[64,1024]{1,0:T(8,128)(2,1)S(1)} %get-tuple-element.675), channel_id=1, source_target_pairs={{0,16},{16,0},{1,17},{17,1},{2,18},{18,2},{3,19},{19,3},{4,20},{20... | collective-permute-start | bytes 393224 | tf_op jit(solution)/shard_map/while/body/eval_jaxpr/ppermute | solution.py:18
  255.4 0.9 constant_dynamic-slice_fusion.8
  257.0 1.4 collective-permute-done.1
  258.5 1.0 bitcast_select_fusion.7
  259.5 40.1 %conditional.5 = (bf16[64,1024]{1,0:T(8,128)(2,1)S(1)}) conditional(s32[]{:T(128)} %convert_element_type.246, bf16[64,1024]{1,0:T(8,128)(2,1)S(1)} %bitcast_select_fusion.7, (bf16[64,1024]{1,0:T(8,128)(2,1)S(1)}, bf16[9216,1024]{1,0:T(8,128)(2,1)}, s32[]{:T(128)}, bf16[2,64,1024]{2,1,0:T(8,128)(2,1)S(1)}, f32[2,2048]{1,0:T(2,128)}) %tuple.118), branch_computations={%region_16.16_spmd, %region_17.27_spmd} | conditional | flops 1212638592 | bytes 25697282 | solution.py:139
  267.2 13.2 %fusion.33 = bf16[1,8,8,9216]{3,2,1,0:T(8,128)(2,1)} fusion(bf16[64,1024]{1,0:T(8,128)(2,1)S(1)} %get-tuple-element.380, bf16[9216,1024]{1,0:T(8,128)(2,1)} %get-tuple-element.381), kind=kOutput, calls=%fused_computation.57 | convolution fusion | flops 1208549376 | bytes 20185088 | tf_op jit(solution)/shard_map/while/body/eval_jaxpr/cond/branch_1_fun/transpose(jvp())/dot_general | solution.py:80
  280.4 2.2 fusion.94
  282.6 0.9 pad_add_fusion
  284.3 3.0 multiply_reduce_fusion
  287.2 1.3 reduce_sum.142
  292.2 1.4 reduce_sum.154
  293.5 1.4 reduce_sum.155
  298.5 1.1 fusion.55
  299.6 2.0 collective-permute-start.1
  301.6 0.9 constant_dynamic-slice_fusion.8
  303.2 1.5 collective-permute-done.1
  304.7 1.0 bitcast_select_fusion.7
  305.7 40.1 %conditional.5 = (bf16[64,1024]{1,0:T(8,128)(2,1)S(1)}) conditional(s32[]{:T(128)} %convert_element_type.246, bf16[64,1024]{1,0:T(8,128)(2,1)S(1)} %bitcast_select_fusion.7, (bf16[64,1024]{1,0:T(8,128)(2,1)S(1)}, bf16[9216,1024]{1,0:T(8,128)(2,1)}, s32[]{:T(128)}, bf16[2,64,1024]{2,1,0:T(8,128)(2,1)S(1)}, f32[2,2048]{1,0:T(2,128)}) %tuple.118), branch_computations={%region_16.16_spmd, %region_17.27_spmd} | conditional | flops 1212638592 | bytes 25697282 | solution.py:139
  313.4 13.2 %fusion.33 = bf16[1,8,8,9216]{3,2,1,0:T(8,128)(2,1)} fusion(bf16[64,1024]{1,0:T(8,128)(2,1)S(1)} %get-tuple-element.380, bf16[9216,1024]{1,0:T(8,128)(2,1)} %get-tuple-element.381), kind=kOutput, calls=%fused_computation.57 | convolution fusion | flops 1208549376 | bytes 20185088 | tf_op jit(solution)/shard_map/while/body/eval_jaxpr/cond/branch_1_fun/transpose(jvp())/dot_general | solution.py:80
  326.6 2.2 fusion.94
  330.5 3.0 multiply_reduce_fusion
  333.5 1.3 reduce_sum.142
  338.4 1.4 reduce_sum.154
  339.7 1.4 reduce_sum.155
  344.7 1.1 fusion.55
  345.9 0.9 constant_dynamic-slice_fusion.8
  347.5 3.4 collective-permute-done.1
  350.9 1.7 broadcast_select_fusion
  353.3 3.3 copy.24
  356.6 3.4 copy.25
  360.0 3.3 copy.26
  363.3 3.4 copy.27
  366.7 14.6 %all-reduce.16.cloned.1.call-done = (bf16[2,64,1024]{2,1,0:T(8,128)(2,1)}, bf16[2,64,1024]{2,1,0:T(8,128)(2,1)}) async-done(((bf16[2,64,1024]{2,1,0:T(8,128)(2,1)}, bf16[2,64,1024]{2,1,0:T(8,128)(2,1)}), (bf16[2,64,1024]{2,1,0:T(8,128)(2,1)}, bf16[2,64,1024]{2,1,0:T(8,128)(2,1)})) %all-reduce.16.cloned.1.call-update) | async-done | bytes 524304 | tf_op jit(solution)/shard_map/psum | solution.py:23
  381.4 3.8 multiply_reduce_fusion.5
  385.2 4.9 %psum.39 = bf16[2,2]{0,1:T(2,128)(2,1)S(1)} all-reduce(bf16[2,2]{0,1:T(2,128)(2,1)S(1)} %pad_maximum_fusion.1), channel_id=1, replica_groups=mesh['section'=2,'batch'=16] {'section'}, use_global_device_ids=true, to_apply=%region_34.35 | all-reduce | flops 4 | bytes 16 | tf_op jit(solution)/shard_map/psum | solution.py:101
  390.8 2.7 fusion.79
  (157 shorter events, 60.5 us)
Async XLA Ops:
  8.0 23.3 %copy-start = (bf16[1024,1536]{1,0:T(8,128)(2,1)S(1)}, bf16[1024,1536]{1,0:T(8,128)(2,1)}, u32[]{:S(2)}) copy-start(bf16[1024,1536]{1,0:T(8,128)(2,1)} %param.28) | copy-start | bytes 9437188
  8.0 56.8 %all-reduce.18.cloned.1.call-start = ((), (), s32[]{:S(2)}) async-start(), calls=%async_computation.2 | async-start | bytes 1048576 | tf_op jit(solution)/shard_map/psum | solution.py:101
  12.0 3.4 copy-start.6
  12.0 3.4 copy-start.7
  22.2 4.0 %copy-start.8 = (s32[2]{0:T(128)S(1)}, s32[2]{0:T(128)}, u32[]{:S(2)}) copy-start(s32[2]{0:T(128)} %param.24) | copy-start | bytes 28
  26.4 4.8 %copy-start.2 = (f32[2]{0:T(128)}, f32[2]{0:T(128)S(1)}, u32[]{:S(2)}) copy-start(f32[2]{0:T(128)S(1)} %get-tuple-element.477) | copy-start | bytes 28
  26.4 4.8 %copy-start.4 = (f32[2]{0:T(128)}, f32[2]{0:T(128)S(1)}, u32[]{:S(2)}) copy-start(f32[2]{0:T(128)S(1)} %get-tuple-element.479) | copy-start | bytes 28
  33.1 103.8 %all-gather.2.cloned.1.call-start = ((), (), s32[]{:S(2)}) async-start(), calls=%async_computation | async-start | bytes 20054016 | tf_op jit(solution)/shard_map/all_gather | solution.py:165
  33.7 347.6 %all-reduce.16.cloned.1.call-start = ((), (), s32[]{:S(2)}) async-start(), calls=%async_computation.1 | async-start | bytes 1048576 | tf_op jit(solution)/shard_map/psum | solution.py:23
  157.6 5.8 %collective-permute-start = (bf16[64,1024]{1,0:T(8,128)(2,1)S(1)}, bf16[64,1024]{1,0:T(8,128)(2,1)}, u32[]{:S(2)}, u32[]{:S(2)}) collective-permute-start(bf16[64,1024]{1,0:T(8,128)(2,1)S(1)} %get-tuple-element.674), channel_id=1, source_target_pairs={{0,16},{16,0},{1,17},{17,1},{2,18},{18,2},{3,19},{19,3},{4,20},{20... | collective-permute-start | bytes 393224 | tf_op jit(solution)/shard_map/while/body/eval_jaxpr/ppermute | solution.py:18
  182.8 5.1 %collective-permute-start = (bf16[64,1024]{1,0:T(8,128)(2,1)S(1)}, bf16[64,1024]{1,0:T(8,128)(2,1)}, u32[]{:S(2)}, u32[]{:S(2)}) collective-permute-start(bf16[64,1024]{1,0:T(8,128)(2,1)S(1)} %get-tuple-element.674), channel_id=1, source_target_pairs={{0,16},{16,0},{1,17},{17,1},{2,18},{18,2},{3,19},{19,3},{4,20},{20... | collective-permute-start | bytes 393224 | tf_op jit(solution)/shard_map/while/body/eval_jaxpr/ppermute | solution.py:18
  188.9 22.0 %collective-permute-start = (bf16[64,1024]{1,0:T(8,128)(2,1)S(1)}, bf16[64,1024]{1,0:T(8,128)(2,1)}, u32[]{:S(2)}, u32[]{:S(2)}) collective-permute-start(bf16[64,1024]{1,0:T(8,128)(2,1)S(1)} %get-tuple-element.674), channel_id=1, source_target_pairs={{0,16},{16,0},{1,17},{17,1},{2,18},{18,2},{3,19},{19,3},{4,20},{20... | collective-permute-start | bytes 393224 | tf_op jit(solution)/shard_map/while/body/eval_jaxpr/ppermute | solution.py:18
  213.3 45.2 %collective-permute-start.1 = (bf16[64,1024]{1,0:T(8,128)(2,1)S(1)}, bf16[64,1024]{1,0:T(8,128)(2,1)}, u32[]{:S(2)}, u32[]{:S(2)}) collective-permute-start(bf16[64,1024]{1,0:T(8,128)(2,1)S(1)} %get-tuple-element.675), channel_id=1, source_target_pairs={{0,16},{16,0},{1,17},{17,1},{2,18},{18,2},{3,19},{19,3},{4,20},{20... | collective-permute-start | bytes 393224 | tf_op jit(solution)/shard_map/while/body/eval_jaxpr/ppermute | solution.py:18
  265.2 0.5 copy-start.1
  299.6 5.1 %collective-permute-start.1 = (bf16[64,1024]{1,0:T(8,128)(2,1)S(1)}, bf16[64,1024]{1,0:T(8,128)(2,1)}, u32[]{:S(2)}, u32[]{:S(2)}) collective-permute-start(bf16[64,1024]{1,0:T(8,128)(2,1)S(1)} %get-tuple-element.675), channel_id=1, source_target_pairs={{0,16},{16,0},{1,17},{17,1},{2,18},{18,2},{3,19},{19,3},{4,20},{20... | collective-permute-start | bytes 393224 | tf_op jit(solution)/shard_map/while/body/eval_jaxpr/ppermute | solution.py:18
  311.4 0.5 copy-start.1
  345.8 5.1 %collective-permute-start.1 = (bf16[64,1024]{1,0:T(8,128)(2,1)S(1)}, bf16[64,1024]{1,0:T(8,128)(2,1)}, u32[]{:S(2)}, u32[]{:S(2)}) collective-permute-start(bf16[64,1024]{1,0:T(8,128)(2,1)S(1)} %get-tuple-element.675), channel_id=1, source_target_pairs={{0,16},{16,0},{1,17},{17,1},{2,18},{18,2},{3,19},{19,3},{4,20},{20... | collective-permute-start | bytes 393224 | tf_op jit(solution)/shard_map/while/body/eval_jaxpr/ppermute | solution.py:18
  363.3 18.0 %copy-start.3 = (f32[2]{0:T(128)S(1)}, f32[2]{0:T(128)}, u32[]{:S(2)}) copy-start(f32[2]{0:T(128)} %copy-done.2) | copy-start | bytes 28
  381.4 9.4 %copy-start.5 = (f32[2]{0:T(128)S(1)}, f32[2]{0:T(128)}, u32[]{:S(2)}) copy-start(f32[2]{0:T(128)} %copy-done.4) | copy-start | bytes 28
Sparse Core Ops, SparseCore 0:
  33.3 31.5 all-reduce.17
  353.5 27.8 all-reduce.15
Sparse Core Ops, SparseCore 1:
  35.3 101.6 all-gather.1
where the time goes:
time: 404 us; the launch traced here: 401 us
  waiting for transfers between devices  130 us (32%)
  local copies, waits for them, and re-layouts  72.5 us (18%)
  starting transfers between devices  63.8 us (16%)
  matrix products  61.1 us (15%)
  other arithmetic  52.8 us (13%)
  between operations  15.6 us (4%)
  blocking collectives  4.94 us (1%)
    all_gather x1, waiting for transfers between devices, local(): full_conv = lax.all_gather(conv_weight, 'batch', axis=1, tiled=True)[0]  72.1 us
    ppermute x6, starting transfers between devices, shifted(): return lax.ppermute(value, axis, pairs)  63.6 us
    dot_general x4, matrix products, conv_branch(): product = jnp.dot(columns, weight, preferred_element_type=jnp.float32)  46.1 us
    psum x1, waiting for transfers between devices, section_total(): lax.psum(partial_sum.astype(jnp.bfloat16), 'section').astype(jnp.float32)  27.4 us
    reduce_sum x5, local copies, waits for them, and re-layouts, apply_map(): jnp.sum(matrix[:, None, None, :, :] * pixels[:, :, :, None, :], axis=-1)  16.7 us
    ppermute x6, waiting for transfers between devices, shifted(): return lax.ppermute(value, axis, pairs)  15.1 us
    psum x1, waiting for transfers between devices, from_root(): return lax.psum(block, axis)  14.6 us
    reduce_sum x8, other arithmetic, conv_branch(): grouped - centre  11.6 us
  transfers between devices with their start and end apart: 9, of which 9 were waited for; matrix products, arithmetic and copies ran while one was open for 7% of the time, Pallas kernels for 0%

commit v1 on v0

--- a/solution.py
+++ b/solution.py
@@ -10,6 +10,22 @@
 GRID = 8
 TSTEPS = 1000
 PV = 3072
+
+
+def gather_around(x, axis, dim):
+    ways, here, hop = (lax.axis_size(axis), lax.axis_index(axis), x.shape[dim])
+    lengths = [n * ways if d == dim else n for d, n in enumerate(x.shape)]
+    full = lax.dynamic_update_slice_in_dim(jnp.zeros(lengths, x.dtype), x, here * hop, axis=dim)
+    going_up = going_down = x
+    for far in range(1, ways // 2 + 1):
+        going_up = lax.ppermute(going_up, axis, [(d, (d + 1) % ways) for d in range(ways)])
+        full = lax.dynamic_update_slice_in_dim(full, going_up, (here - far) % ways * hop, axis=dim)
+        if 2 * far < ways:
+            going_down = lax.ppermute(going_down, axis, [(d, (d - 1) % ways) for d in range(ways)])
+            full = lax.dynamic_update_slice_in_dim(
+                full, going_down, (here + far) % ways * hop, axis=dim
+            )
+    return full
 
 
 def shifted(value, axis, steps):
@@ -162,7 +178,7 @@
     place = lax.axis_index("section")
     number = images.shape[0]
     columns_here = images.shape[2]
-    full_conv = lax.all_gather(conv_weight, "batch", axis=1, tiled=True)[0]
+    full_conv = gather_around(conv_weight, "batch", 1)[0]
     level = noise_levels(timestep)
     root_level = jnp.sqrt(level)[:, None, None]
     root_noise = jnp.sqrt(1.0 - level)[:, None, None]

time: 404 us -> 491 us (1.22)
  starting transfers between devices: 63.8 us -> 172 us
  waiting for transfers between devices: 130 us -> 70.8 us
  local copies, waits for them, and re-layouts: 72.5 us -> 111 us
    ppermute x0 -> x15, starting transfers between devices: none -> 109 us  [the longest x8 99.2 us: gather_around(): lax.ppermute(going_up, axis, [(d, (d + 1) % ways) for d in range(ways)])]
    all_gather x1 -> x0, waiting for transfers between devices: 72.1 us -> none  [local(): full_conv = lax.all_gather(conv_weight, 'batch', axis=1, tiled=True)[0]]
    ppermute x0 -> x15, waiting for transfers between devices: none -> 32 us  [the longest x8 32 us: gather_around(): lax.ppermute(going_up, axis, [(d, (d + 1) % ways) for d in range(ways)])]
    dynamic_update_slice x0 -> x16, local copies, waits for them, and re-layouts: none -> 31.9 us  [the longest x8 16.6 us: gather_around(): lax.dynamic_update_slice_in_dim(full, going_up, (here - far) % ways * hop...]
    psum x1, waiting for transfers between devices: 27.4 us -> 0.01 us  [section_total(): lax.psum(partial_sum.astype(jnp.bfloat16), 'section').astype(jnp.float32)]
    psum x1, waiting for transfers between devices: 14.6 us -> 24 us  [from_root(): return lax.psum(block, axis)]
    squeeze x0 -> x1, local copies, waits for them, and re-layouts: none -> 6.74 us  [local(): full_conv = gather_around(conv_weight, 'batch', 1)[0]]
  transfers between devices with their start and end apart: 9 -> 23, of which waited for: 9 -> 11; matrix products, arithmetic and copies ran while one was open for 7% -> 18% of each run, Pallas kernels for 0% -> 0%
where the time goes in v1:
time: 491 us; the launch traced here: 488 us
  starting transfers between devices  172 us (35%)
  local copies, waits for them, and re-layouts  111 us (23%)
  waiting for transfers between devices  70.8 us (14%)
  matrix products  61 us (12%)
  other arithmetic  53.5 us (11%)
  between operations  14.2 us (3%)
  blocking collectives  4.94 us (1%)
    ppermute x8, starting transfers between devices, gather_around(): lax.ppermute(going_up, axis, [(d, (d + 1) % ways) for d in range(ways)])  99.2 us
    ppermute x6, starting transfers between devices, shifted(): return lax.ppermute(value, axis, pairs)  62.9 us
    dot_general x4, matrix products, conv_branch(): product = jnp.dot(columns, weight, preferred_element_type=jnp.float32)  46.1 us
    ppermute x8, waiting for transfers between devices, gather_around(): lax.ppermute(going_up, axis, [(d, (d + 1) % ways) for d in range(ways)])  32 us
    psum x1, waiting for transfers between devices, from_root(): return lax.psum(block, axis)  24 us
    reduce_sum x5, local copies, waits for them, and re-layouts, apply_map(): jnp.sum(matrix[:, None, None, :, :] * pixels[:, :, :, None, :], axis=-1)  16.8 us
    dynamic_update_slice x8, local copies, waits for them, and re-layouts, gather_around(): lax.dynamic_update_slice_in_dim(full, going_up, (here - far) % ways * hop...  16.6 us
    ppermute x6, waiting for transfers between devices, shifted(): return lax.ppermute(value, axis, pairs)  14.7 us
  transfers between devices with their start and end apart: 23, of which 11 were waited for; matrix products, arithmetic and copies ran while one was open for 18% of the time, Pallas kernels for 0%

profile of v1, /device:TPU:0, one launch (start us, length us, event | category | flops | bytes accessed | tf_op | source)
XLA Modules:
  0.0 487.9 jit_solution(17865519318619300279)
XLA Ops:
  7.8 5.0 %collective-permute-start.3 = (bf16[1,576,1024]{2,1,0:T(8,128)(2,1)}, bf16[1,576,1024]{2,1,0:T(8,128)(2,1)}, u32[]{:S(2)}, u32[]{:S(2)}) collective-permute-start(bf16[1,576,1024]{2,1,0:T(8,128)(2,1)} %param.26), channel_id=1, source_target_pairs={{0,15},{1,0},{2,1},{3,2},{4,3},{5,4},{6,5},{7,6},{8,7},{9,8},{10,9... | collective-permute-start | bytes 3538952 | tf_op jit(solution)/shard_map/ppermute | solution.py:24
  12.8 14.1 %collective-permute-done.2 = bf16[1,576,1024]{2,1,0:T(8,128)(2,1)S(1)} collective-permute-done((bf16[1,576,1024]{2,1,0:T(8,128)(2,1)}, bf16[1,576,1024]{2,1,0:T(8,128)(2,1)S(1)}, u32[]{:S(2)}, u32[]{:S(2)}) %collective-permute-start.2) | collective-permute-done | bytes 1179680 | tf_op jit(solution)/shard_map/ppermute | solution.py:21
  28.0 9.5 %collective-permute-start.4 = (bf16[1,576,1024]{2,1,0:T(8,128)(2,1)S(1)}, bf16[1,576,1024]{2,1,0:T(8,128)(2,1)}, u32[]{:S(2)}, u32[]{:S(2)}) collective-permute-start(bf16[1,576,1024]{2,1,0:T(8,128)(2,1)S(1)} %collective-permute-done.2), channel_id=1, source_target_pairs={{0,1},{1,2},{2,3},{3,4},{4,5},{5,6},{6,7},{7,8},{8,9},{9,10},{10,1... | collective-permute-start | bytes 3538952 | tf_op jit(solution)/shard_map/ppermute | solution.py:21
  37.5 9.0 %collective-permute-done.4 = bf16[1,576,1024]{2,1,0:T(8,128)(2,1)} collective-permute-done((bf16[1,576,1024]{2,1,0:T(8,128)(2,1)S(1)}, bf16[1,576,1024]{2,1,0:T(8,128)(2,1)}, u32[]{:S(2)}, u32[]{:S(2)}) %collective-permute-start.4) | collective-permute-done | bytes 1179680 | tf_op jit(solution)/shard_map/ppermute | solution.py:21
  46.5 18.7 %collective-permute-start.6 = (bf16[1,576,1024]{2,1,0:T(8,128)(2,1)}, bf16[1,576,1024]{2,1,0:T(8,128)(2,1)}, u32[]{:S(2)}, u32[]{:S(2)}) collective-permute-start(bf16[1,576,1024]{2,1,0:T(8,128)(2,1)} %collective-permute-done.4), channel_id=1, source_target_pairs={{0,1},{1,2},{2,3},{3,4},{4,5},{5,6},{6,7},{7,8},{8,9},{9,10},{10,1... | collective-permute-start | bytes 3538952 | tf_op jit(solution)/shard_map/ppermute | solution.py:21
  65.2 3.0 copy.20
  68.2 3.4 copy.21
  71.8 3.5 multiply_reduce_fusion.2
  75.3 3.3 copy.22
  78.6 3.4 copy.23
  82.5 11.4 %collective-permute-start.8 = (bf16[1,576,1024]{2,1,0:T(8,128)(2,1)}, bf16[1,576,1024]{2,1,0:T(8,128)(2,1)}, u32[]{:S(2)}, u32[]{:S(2)}) collective-permute-start(bf16[1,576,1024]{2,1,0:T(8,128)(2,1)} %collective-permute-done.6), channel_id=1, source_target_pairs={{0,1},{1,2},{2,3},{3,4},{4,5},{5,6},{6,7},{7,8},{8,9},{9,10},{10,1... | collective-permute-start | bytes 3538952 | tf_op jit(solution)/shard_map/ppermute | solution.py:21
  95.1 1.5 fusion.82
  96.6 8.4 %collective-permute-done.8 = bf16[1,576,1024]{2,1,0:T(8,128)(2,1)} collective-permute-done((bf16[1,576,1024]{2,1,0:T(8,128)(2,1)}, bf16[1,576,1024]{2,1,0:T(8,128)(2,1)}, u32[]{:S(2)}, u32[]{:S(2)}) %collective-permute-start.8) | collective-permute-done | bytes 1179680 | tf_op jit(solution)/shard_map/ppermute | solution.py:21
  105.0 17.5 %collective-permute-start.10 = (bf16[1,576,1024]{2,1,0:T(8,128)(2,1)}, bf16[1,576,1024]{2,1,0:T(8,128)(2,1)}, u32[]{:S(2)}, u32[]{:S(2)}) collective-permute-start(bf16[1,576,1024]{2,1,0:T(8,128)(2,1)} %collective-permute-done.8), channel_id=1, source_target_pairs={{0,1},{1,2},{2,3},{3,4},{4,5},{5,6},{6,7},{7,8},{8,9},{9,10},{10,1... | collective-permute-start | bytes 3538952 | tf_op jit(solution)/shard_map/ppermute | solution.py:21
  122.5 3.2 convolution_convert_fusion.2
  125.7 1.8 convolution_convert_fusion.1
  127.9 3.4 fusion.58
  131.3 19.8 %collective-permute-start.12 = (bf16[1,576,1024]{2,1,0:T(8,128)(2,1)}, bf16[1,576,1024]{2,1,0:T(8,128)(2,1)}, u32[]{:S(2)}, u32[]{:S(2)}) collective-permute-start(bf16[1,576,1024]{2,1,0:T(8,128)(2,1)} %collective-permute-done.10), channel_id=1, source_target_pairs={{0,1},{1,2},{2,3},{3,4},{4,5},{5,6},{6,7},{7,8},{8,9},{9,10},{10,1... | collective-permute-start | bytes 3538952 | tf_op jit(solution)/shard_map/ppermute | solution.py:21
  151.1 6.7 %squeeze.82 = bf16[9216,1024]{1,0:T(8,128)(2,1)} broadcast(bf16[]{:T(256)} %constant.279.clone.1), dimensions={} | broadcast | bytes 18874370 | tf_op jit(solution)/shard_map/squeeze | solution.py:181
  158.9 2.4 bitcast_dynamic-update-slice_fusion.17
  161.3 2.4 bitcast_dynamic-update-slice_fusion.16
  163.7 2.4 bitcast_dynamic-update-slice_fusion.15
  166.1 2.4 bitcast_dynamic-update-slice_fusion.14
  168.5 2.4 collective-permute-start.14
  170.9 2.4 bitcast_dynamic-update-slice_fusion.13
  173.3 2.3 bitcast_dynamic-update-slice_fusion.12
  175.7 2.4 bitcast_dynamic-update-slice_fusion.11
  178.1 2.4 bitcast_dynamic-update-slice_fusion.10
  180.5 4.3 collective-permute-start.15
  184.8 2.4 bitcast_dynamic-update-slice_fusion.9
  187.2 19.3 %collective-permute-start.16 = (bf16[1,576,1024]{2,1,0:T(8,128)(2,1)S(1)}, bf16[1,576,1024]{2,1,0:T(8,128)(2,1)S(1)}, u32[]{:S(2)}, u32[]{:S(2)}) collective-permute-start(bf16[1,576,1024]{2,1,0:T(8,128)(2,1)S(1)} %collective-permute-done.14), channel_id=1, source_target_pairs={{0,1},{1,2},{2,3},{3,4},{4,5},{5,6},{6,7},{7,8},{8,9},{9,10},{10,1... | collective-permute-start | bytes 3538952 | tf_op jit(solution)/shard_map/ppermute | solution.py:21
  206.5 2.4 bitcast_dynamic-update-slice_fusion.8
  208.9 2.4 bitcast_dynamic-update-slice_fusion.7
  217.6 71.4 %while.34 = (s32[]{:T(128)}, bf16[64,1024]{1,0:T(8,128)(2,1)}, bf16[2,64,1024]{2,1,0:T(8,128)(2,1)S(1)}, bf16[2,64,1024]{2,1,0:T(8,128)(2,1)}, s32[]{:T(128)}, /...) while((s32[]{:T(128)}, bf16[64,1024]{1,0:T(8,128)(2,1)}, ...), condition=%wide.region_12.13_spmd, body=%wide.region_5.12_spmd.sunk | while | flops 1210057728 | bytes 25409360 | solution.py:161
  218.6 18.3 %conditional.4 = (bf16[64,1024]{1,0:T(8,128)(2,1)S(1)}) conditional(s32[]{:T(128)} %convert_element_type.245, bf16[64,1024]{1,0:T(8,128)(2,1)S(1)} %get-tuple-element.587, (bf16[64,1024]{1,0:T(8,128)(2,1)S(1)}, s32[]{:T(128)}, f32[2,2048]{1,0:T(2,128)}, bf16[9216,1024]{1,0:T(8,128)(2,1)}) %tuple.116), branch_computations={%region_6.6_spmd, %region_7.11_spmd} | conditional | flops 1209861120 | bytes 23311430 | solution.py:155
  227.1 9.8 %fusion = bf16[64,1024]{1,0:T(8,128)(2,1)S(1)} fusion(bf16[64,9216]{1,0:T(8,128)(2,1)S(1)} %fusion.32, bf16[9216,1024]{1,0:T(8,128)(2,1)} %get-tuple-element.369, bf16[64,1024]{1,0:T(8,128)(2,1)S(1)} %get-tuple-element.366), kind=kOutput, calls=%fused_computation.1 | convolution fusion | flops 1208156160 | bytes 20316160 | tf_op jit(solution)/shard_map/while/body/eval_jaxpr/cond/branch_1_fun/dot_general | solution.py:96
  238.6 3.4 collective-permute-done
  243.0 18.3 %conditional.4 = (bf16[64,1024]{1,0:T(8,128)(2,1)S(1)}) conditional(s32[]{:T(128)} %convert_element_type.245, bf16[64,1024]{1,0:T(8,128)(2,1)S(1)} %get-tuple-element.587, (bf16[64,1024]{1,0:T(8,128)(2,1)S(1)}, s32[]{:T(128)}, f32[2,2048]{1,0:T(2,128)}, bf16[9216,1024]{1,0:T(8,128)(2,1)}) %tuple.116), branch_computations={%region_6.6_spmd, %region_7.11_spmd} | conditional | flops 1209861120 | bytes 23311430 | solution.py:155
  251.5 9.8 %fusion = bf16[64,1024]{1,0:T(8,128)(2,1)S(1)} fusion(bf16[64,9216]{1,0:T(8,128)(2,1)S(1)} %fusion.32, bf16[9216,1024]{1,0:T(8,128)(2,1)} %get-tuple-element.369, bf16[64,1024]{1,0:T(8,128)(2,1)S(1)} %get-tuple-element.366), kind=kOutput, calls=%fused_computation.1 | convolution fusion | flops 1208156160 | bytes 20316160 | tf_op jit(solution)/shard_map/while/body/eval_jaxpr/cond/branch_1_fun/dot_general | solution.py:96
  263.1 3.4 collective-permute-done
  267.5 18.5 %collective-permute-start = (bf16[64,1024]{1,0:T(8,128)(2,1)S(1)}, bf16[64,1024]{1,0:T(8,128)(2,1)}, u32[]{:S(2)}, u32[]{:S(2)}) collective-permute-start(bf16[64,1024]{1,0:T(8,128)(2,1)S(1)} %get-tuple-element.674), channel_id=1, source_target_pairs={{0,16},{16,0},{1,17},{17,1},{2,18},{18,2},{3,19},{19,3},{4,20},{20... | collective-permute-start | bytes 393224 | tf_op jit(solution)/shard_map/while/body/eval_jaxpr/ppermute | solution.py:34
  290.4 138.8 %while.35 = (s32[]{:T(128)}, bf16[64,1024]{1,0:T(8,128)(2,1)}, bf16[2,64,1024]{2,1,0:T(8,128)(2,1)}, s32[]{:T(128)}, pred[]{:T(512)}, /*index=5*/bf16[2,64,1024]...) while((s32[]{:T(128)}, bf16[64,1024]{1,0:T(8,128)(2,1)}, ...), condition=%wide.region_28.29_spmd, body=%wide.region_15.28_spmd.sunk | while | flops 1212769664 | bytes 27270924 | solution.py:161
  291.4 42.2 %collective-permute-start.1 = (bf16[64,1024]{1,0:T(8,128)(2,1)S(1)}, bf16[64,1024]{1,0:T(8,128)(2,1)}, u32[]{:S(2)}, u32[]{:S(2)}) collective-permute-start(bf16[64,1024]{1,0:T(8,128)(2,1)S(1)} %get-tuple-element.675), channel_id=1, source_target_pairs={{0,16},{16,0},{1,17},{17,1},{2,18},{18,2},{3,19},{19,3},{4,20},{20... | collective-permute-start | bytes 393224 | tf_op jit(solution)/shard_map/while/body/eval_jaxpr/ppermute | solution.py:34
  335.2 1.5 collective-permute-done.1
  337.6 40.2 %conditional.5 = (bf16[64,1024]{1,0:T(8,128)(2,1)S(1)}) conditional(s32[]{:T(128)} %convert_element_type.246, bf16[64,1024]{1,0:T(8,128)(2,1)S(1)} %bitcast_select_fusion.7, (bf16[64,1024]{1,0:T(8,128)(2,1)S(1)}, bf16[9216,1024]{1,0:T(8,128)(2,1)}, s32[]{:T(128)}, bf16[2,64,1024]{2,1,0:T(8,128)(2,1)S(1)}, f32[2,2048]{1,0:T(2,128)}) %tuple.118), branch_computations={%region_16.16_spmd, %region_17.27_spmd} | conditional | flops 1212638592 | bytes 25697282 | solution.py:155
  345.3 13.2 %fusion.33 = bf16[1,8,8,9216]{3,2,1,0:T(8,128)(2,1)} fusion(bf16[64,1024]{1,0:T(8,128)(2,1)S(1)} %get-tuple-element.380, bf16[9216,1024]{1,0:T(8,128)(2,1)} %get-tuple-element.381), kind=kOutput, calls=%fused_computation.57 | convolution fusion | flops 1208549376 | bytes 20185088 | tf_op jit(solution)/shard_map/while/body/eval_jaxpr/cond/branch_1_fun/transpose(jvp())/dot_general | solution.py:96
  358.5 2.2 fusion.94
  362.4 3.0 multiply_reduce_fusion
  377.8 2.0 collective-permute-start.1
  381.4 1.5 collective-permute-done.1
  383.9 40.2 %conditional.5 = (bf16[64,1024]{1,0:T(8,128)(2,1)S(1)}) conditional(s32[]{:T(128)} %convert_element_type.246, bf16[64,1024]{1,0:T(8,128)(2,1)S(1)} %bitcast_select_fusion.7, (bf16[64,1024]{1,0:T(8,128)(2,1)S(1)}, bf16[9216,1024]{1,0:T(8,128)(2,1)}, s32[]{:T(128)}, bf16[2,64,1024]{2,1,0:T(8,128)(2,1)S(1)}, f32[2,2048]{1,0:T(2,128)}) %tuple.118), branch_computations={%region_16.16_spmd, %region_17.27_spmd} | conditional | flops 1212638592 | bytes 25697282 | solution.py:155
  391.5 13.2 %fusion.33 = bf16[1,8,8,9216]{3,2,1,0:T(8,128)(2,1)} fusion(bf16[64,1024]{1,0:T(8,128)(2,1)S(1)} %get-tuple-element.380, bf16[9216,1024]{1,0:T(8,128)(2,1)} %get-tuple-element.381), kind=kOutput, calls=%fused_computation.57 | convolution fusion | flops 1208549376 | bytes 20185088 | tf_op jit(solution)/shard_map/while/body/eval_jaxpr/cond/branch_1_fun/transpose(jvp())/dot_general | solution.py:96
  404.8 2.2 fusion.94
  408.7 3.0 multiply_reduce_fusion
  425.7 3.5 collective-permute-done.1
  429.2 1.7 broadcast_select_fusion
  431.6 3.3 copy.24
  434.9 3.4 copy.25
  438.3 3.4 copy.26
  441.6 3.4 copy.27
  445.0 24.0 %all-reduce.16.cloned.1.call-done = (bf16[2,64,1024]{2,1,0:T(8,128)(2,1)}, bf16[2,64,1024]{2,1,0:T(8,128)(2,1)}) async-done(((bf16[2,64,1024]{2,1,0:T(8,128)(2,1)}, bf16[2,64,1024]{2,1,0:T(8,128)(2,1)}), (bf16[2,64,1024]{2,1,0:T(8,128)(2,1)}, bf16[2,64,1024]{2,1,0:T(8,128)(2,1)})) %all-reduce.16.cloned.1.call-update) | async-done | bytes 524304 | tf_op jit(solution)/shard_map/psum | solution.py:39
  469.1 3.7 multiply_reduce_fusion.5
  472.8 4.9 %psum.39 = bf16[2,2]{0,1:T(2,128)(2,1)S(1)} all-reduce(bf16[2,2]{0,1:T(2,128)(2,1)S(1)} %pad_maximum_fusion.1), channel_id=1, replica_groups=mesh['section'=2,'batch'=16] {'section'}, use_global_device_ids=true, to_apply=%region_34.35 | all-reduce | flops 4 | bytes 16 | tf_op jit(solution)/shard_map/psum | solution.py:117
  478.4 2.7 fusion.79
  (211 shorter events, 91.2 us)
Async XLA Ops:
  7.2 118.5 %copy-start = (bf16[1024,1536]{1,0:T(8,128)(2,1)S(1)}, bf16[1024,1536]{1,0:T(8,128)(2,1)}, u32[]{:S(2)}) copy-start(bf16[1024,1536]{1,0:T(8,128)(2,1)} %param.28) | copy-start | bytes 9437188
  7.2 64.5 %copy-start.10 = (f32[3,3]{1,0:T(4,128)S(1)}, f32[3,3]{1,0:T(4,128)}, u32[]{:S(2)}) copy-start(f32[3,3]{1,0:T(4,128)} %constant.332) | copy-start | bytes 112
  7.2 64.4 %copy-start.13 = (f32[2]{0:T(128)S(1)}, f32[2]{0:T(128)}, u32[]{:S(2)}) copy-start(f32[2]{0:T(128)} %param.22) | copy-start | bytes 28
  7.2 64.4 %copy-start.11 = (f32[2]{0:T(128)S(1)}, f32[2]{0:T(128)}, u32[]{:S(2)}) copy-start(f32[2]{0:T(128)} %param.23) | copy-start | bytes 28
  7.2 209.0 %all-reduce.18.cloned.1.call-start = ((), (), s32[]{:S(2)}) async-start(), calls=%async_computation.1 | async-start | bytes 1048576 | tf_op jit(solution)/shard_map/psum | solution.py:117
  7.3 19.7 %collective-permute-start.2 = (bf16[1,576,1024]{2,1,0:T(8,128)(2,1)}, bf16[1,576,1024]{2,1,0:T(8,128)(2,1)S(1)}, u32[]{:S(2)}, u32[]{:S(2)}) collective-permute-start(bf16[1,576,1024]{2,1,0:T(8,128)(2,1)} %param.26), channel_id=1, source_target_pairs={{0,1},{1,2},{2,3},{3,4},{4,5},{5,6},{6,7},{7,8},{8,9},{9,10},{10,1... | collective-permute-start | bytes 3538952 | tf_op jit(solution)/shard_map/ppermute | solution.py:21
  7.8 29.7 %collective-permute-start.3 = (bf16[1,576,1024]{2,1,0:T(8,128)(2,1)}, bf16[1,576,1024]{2,1,0:T(8,128)(2,1)}, u32[]{:S(2)}, u32[]{:S(2)}) collective-permute-start(bf16[1,576,1024]{2,1,0:T(8,128)(2,1)} %param.26), channel_id=1, source_target_pairs={{0,15},{1,0},{2,1},{3,2},{4,3},{5,4},{6,5},{7,6},{8,7},{9,8},{10,9... | collective-permute-start | bytes 3538952 | tf_op jit(solution)/shard_map/ppermute | solution.py:24
  26.9 1.0 copy-start.4
  28.0 18.5 %collective-permute-start.4 = (bf16[1,576,1024]{2,1,0:T(8,128)(2,1)S(1)}, bf16[1,576,1024]{2,1,0:T(8,128)(2,1)}, u32[]{:S(2)}, u32[]{:S(2)}) collective-permute-start(bf16[1,576,1024]{2,1,0:T(8,128)(2,1)S(1)} %collective-permute-done.2), channel_id=1, source_target_pairs={{0,1},{1,2},{2,3},{3,4},{4,5},{5,6},{6,7},{7,8},{8,9},{9,10},{10,1... | collective-permute-start | bytes 3538952 | tf_op jit(solution)/shard_map/ppermute | solution.py:21
  37.5 34.2 %collective-permute-start.5 = (bf16[1,576,1024]{2,1,0:T(8,128)(2,1)}, bf16[1,576,1024]{2,1,0:T(8,128)(2,1)}, u32[]{:S(2)}, u32[]{:S(2)}) collective-permute-start(bf16[1,576,1024]{2,1,0:T(8,128)(2,1)} %collective-permute-done.3), channel_id=1, source_target_pairs={{0,15},{1,0},{2,1},{3,2},{4,3},{5,4},{6,5},{7,6},{8,7},{9,8},{10,9... | collective-permute-start | bytes 3538952 | tf_op jit(solution)/shard_map/ppermute | solution.py:24
  46.5 36.0 %collective-permute-start.6 = (bf16[1,576,1024]{2,1,0:T(8,128)(2,1)}, bf16[1,576,1024]{2,1,0:T(8,128)(2,1)}, u32[]{:S(2)}, u32[]{:S(2)}) collective-permute-start(bf16[1,576,1024]{2,1,0:T(8,128)(2,1)} %collective-permute-done.4), channel_id=1, source_target_pairs={{0,1},{1,2},{2,3},{3,4},{4,5},{5,6},{6,7},{7,8},{8,9},{9,10},{10,1... | collective-permute-start | bytes 3538952 | tf_op jit(solution)/shard_map/ppermute | solution.py:21
  71.7 23.2 %collective-permute-start.7 = (bf16[1,576,1024]{2,1,0:T(8,128)(2,1)}, bf16[1,576,1024]{2,1,0:T(8,128)(2,1)}, u32[]{:S(2)}, u32[]{:S(2)}) collective-permute-start(bf16[1,576,1024]{2,1,0:T(8,128)(2,1)} %collective-permute-done.5), channel_id=1, source_target_pairs={{0,15},{1,0},{2,1},{3,2},{4,3},{5,4},{6,5},{7,6},{8,7},{9,8},{10,9... | collective-permute-start | bytes 3538952 | tf_op jit(solution)/shard_map/ppermute | solution.py:24
  75.3 19.8 %copy-start.1 = (bf16[2,64,1536]{2,1,0:T(8,128)(2,1)S(1)}, bf16[2,64,1536]{2,1,0:T(8,128)(2,1)}, u32[]{:S(2)}) copy-start(bf16[2,64,1536]{2,1,0:T(8,128)(2,1)} %param.21) | copy-start | bytes 1179652
  82.5 22.5 %collective-permute-start.8 = (bf16[1,576,1024]{2,1,0:T(8,128)(2,1)}, bf16[1,576,1024]{2,1,0:T(8,128)(2,1)}, u32[]{:S(2)}, u32[]{:S(2)}) collective-permute-start(bf16[1,576,1024]{2,1,0:T(8,128)(2,1)} %collective-permute-done.6), channel_id=1, source_target_pairs={{0,1},{1,2},{2,3},{3,4},{4,5},{5,6},{6,7},{7,8},{8,9},{9,10},{10,1... | collective-permute-start | bytes 3538952 | tf_op jit(solution)/shard_map/ppermute | solution.py:21
  94.9 30.7 %copy-start.6 = (f32[2]{0:T(128)}, f32[2]{0:T(128)S(1)}, u32[]{:S(2)}) copy-start(f32[2]{0:T(128)S(1)} %get-tuple-element.477) | copy-start | bytes 28
  95.0 30.7 %copy-start.8 = (f32[2]{0:T(128)}, f32[2]{0:T(128)S(1)}, u32[]{:S(2)}) copy-start(f32[2]{0:T(128)S(1)} %get-tuple-element.479) | copy-start | bytes 28
  95.0 32.8 %collective-permute-start.9 = (bf16[1,576,1024]{2,1,0:T(8,128)(2,1)}, bf16[1,576,1024]{2,1,0:T(8,128)(2,1)}, u32[]{:S(2)}, u32[]{:S(2)}) collective-permute-start(bf16[1,576,1024]{2,1,0:T(8,128)(2,1)} %collective-permute-done.7), channel_id=1, source_target_pairs={{0,15},{1,0},{2,1},{3,2},{4,3},{5,4},{6,5},{7,6},{8,7},{9,8},{10,9... | collective-permute-start | bytes 3538952 | tf_op jit(solution)/shard_map/ppermute | solution.py:24
  105.0 26.3 %collective-permute-start.10 = (bf16[1,576,1024]{2,1,0:T(8,128)(2,1)}, bf16[1,576,1024]{2,1,0:T(8,128)(2,1)}, u32[]{:S(2)}, u32[]{:S(2)}) collective-permute-start(bf16[1,576,1024]{2,1,0:T(8,128)(2,1)} %collective-permute-done.8), channel_id=1, source_target_pairs={{0,1},{1,2},{2,3},{3,4},{4,5},{5,6},{6,7},{7,8},{8,9},{9,10},{10,1... | collective-permute-start | bytes 3538952 | tf_op jit(solution)/shard_map/ppermute | solution.py:21
  125.7 1.9 copy-start.12
  127.5 341.5 %all-reduce.16.cloned.1.call-start = ((), (), s32[]{:S(2)}) async-start(), calls=%async_computation | async-start | bytes 1048576 | tf_op jit(solution)/shard_map/psum | solution.py:39
  127.8 38.3 %collective-permute-start.11 = (bf16[1,576,1024]{2,1,0:T(8,128)(2,1)}, bf16[1,576,1024]{2,1,0:T(8,128)(2,1)}, u32[]{:S(2)}, u32[]{:S(2)}) collective-permute-start(bf16[1,576,1024]{2,1,0:T(8,128)(2,1)} %collective-permute-done.9), channel_id=1, source_target_pairs={{0,15},{1,0},{2,1},{3,2},{4,3},{5,4},{6,5},{7,6},{8,7},{9,8},{10,9... | collective-permute-start | bytes 3538952 | tf_op jit(solution)/shard_map/ppermute | solution.py:24
  131.3 26.5 %copy-start.3 = (bf16[1,576,1024]{2,1,0:T(8,128)(2,1)S(1)}, bf16[1,576,1024]{2,1,0:T(8,128)(2,1)}, u32[]{:S(2)}) copy-start(bf16[1,576,1024]{2,1,0:T(8,128)(2,1)} %param.26) | copy-start | bytes 3538948
  131.3 37.2 %collective-permute-start.12 = (bf16[1,576,1024]{2,1,0:T(8,128)(2,1)}, bf16[1,576,1024]{2,1,0:T(8,128)(2,1)}, u32[]{:S(2)}, u32[]{:S(2)}) collective-permute-start(bf16[1,576,1024]{2,1,0:T(8,128)(2,1)} %collective-permute-done.10), channel_id=1, source_target_pairs={{0,1},{1,2},{2,3},{3,4},{4,5},{5,6},{6,7},{7,8},{8,9},{9,10},{10,1... | collective-permute-start | bytes 3538952 | tf_op jit(solution)/shard_map/ppermute | solution.py:21
  166.1 14.4 %collective-permute-start.13 = (bf16[1,576,1024]{2,1,0:T(8,128)(2,1)}, bf16[1,576,1024]{2,1,0:T(8,128)(2,1)S(1)}, u32[]{:S(2)}, u32[]{:S(2)}) collective-permute-start(bf16[1,576,1024]{2,1,0:T(8,128)(2,1)} %collective-permute-done.11), channel_id=1, source_target_pairs={{0,15},{1,0},{2,1},{3,2},{4,3},{5,4},{6,5},{7,6},{8,7},{9,8},{10,9... | collective-permute-start | bytes 3538952 | tf_op jit(solution)/shard_map/ppermute | solution.py:24
  168.5 18.7 %collective-permute-start.14 = (bf16[1,576,1024]{2,1,0:T(8,128)(2,1)}, bf16[1,576,1024]{2,1,0:T(8,128)(2,1)S(1)}, u32[]{:S(2)}, u32[]{:S(2)}) collective-permute-start(bf16[1,576,1024]{2,1,0:T(8,128)(2,1)} %collective-permute-done.12), channel_id=1, source_target_pairs={{0,1},{1,2},{2,3},{3,4},{4,5},{5,6},{6,7},{7,8},{8,9},{9,10},{10,1... | collective-permute-start | bytes 3538952 | tf_op jit(solution)/shard_map/ppermute | solution.py:21
  180.5 33.0 %collective-permute-start.15 = (bf16[1,576,1024]{2,1,0:T(8,128)(2,1)S(1)}, bf16[1,576,1024]{2,1,0:T(8,128)(2,1)S(1)}, u32[]{:S(2)}, u32[]{:S(2)}) collective-permute-start(bf16[1,576,1024]{2,1,0:T(8,128)(2,1)S(1)} %collective-permute-done.13), channel_id=1, source_target_pairs={{0,15},{1,0},{2,1},{3,2},{4,3},{5,4},{6,5},{7,6},{8,7},{9,8},{10,9... | collective-permute-start | bytes 3538952 | tf_op jit(solution)/shard_map/ppermute | solution.py:24
  187.2 27.9 %collective-permute-start.16 = (bf16[1,576,1024]{2,1,0:T(8,128)(2,1)S(1)}, bf16[1,576,1024]{2,1,0:T(8,128)(2,1)S(1)}, u32[]{:S(2)}, u32[]{:S(2)}) collective-permute-start(bf16[1,576,1024]{2,1,0:T(8,128)(2,1)S(1)} %collective-permute-done.14), channel_id=1, source_target_pairs={{0,1},{1,2},{2,3},{3,4},{4,5},{5,6},{6,7},{7,8},{8,9},{9,10},{10,1... | collective-permute-start | bytes 3538952 | tf_op jit(solution)/shard_map/ppermute | solution.py:21
  236.9 5.1 %collective-permute-start = (bf16[64,1024]{1,0:T(8,128)(2,1)S(1)}, bf16[64,1024]{1,0:T(8,128)(2,1)}, u32[]{:S(2)}, u32[]{:S(2)}) collective-permute-start(bf16[64,1024]{1,0:T(8,128)(2,1)S(1)} %get-tuple-element.674), channel_id=1, source_target_pairs={{0,16},{16,0},{1,17},{17,1},{2,18},{18,2},{3,19},{19,3},{4,20},{20... | collective-permute-start | bytes 393224 | tf_op jit(solution)/shard_map/while/body/eval_jaxpr/ppermute | solution.py:34
  261.3 5.1 %collective-permute-start = (bf16[64,1024]{1,0:T(8,128)(2,1)S(1)}, bf16[64,1024]{1,0:T(8,128)(2,1)}, u32[]{:S(2)}, u32[]{:S(2)}) collective-permute-start(bf16[64,1024]{1,0:T(8,128)(2,1)S(1)} %get-tuple-element.674), channel_id=1, source_target_pairs={{0,16},{16,0},{1,17},{17,1},{2,18},{18,2},{3,19},{19,3},{4,20},{20... | collective-permute-start | bytes 393224 | tf_op jit(solution)/shard_map/while/body/eval_jaxpr/ppermute | solution.py:34
  267.5 21.5 %collective-permute-start = (bf16[64,1024]{1,0:T(8,128)(2,1)S(1)}, bf16[64,1024]{1,0:T(8,128)(2,1)}, u32[]{:S(2)}, u32[]{:S(2)}) collective-permute-start(bf16[64,1024]{1,0:T(8,128)(2,1)S(1)} %get-tuple-element.674), channel_id=1, source_target_pairs={{0,16},{16,0},{1,17},{17,1},{2,18},{18,2},{3,19},{19,3},{4,20},{20... | collective-permute-start | bytes 393224 | tf_op jit(solution)/shard_map/while/body/eval_jaxpr/ppermute | solution.py:34
  291.4 45.2 %collective-permute-start.1 = (bf16[64,1024]{1,0:T(8,128)(2,1)S(1)}, bf16[64,1024]{1,0:T(8,128)(2,1)}, u32[]{:S(2)}, u32[]{:S(2)}) collective-permute-start(bf16[64,1024]{1,0:T(8,128)(2,1)S(1)} %get-tuple-element.675), channel_id=1, source_target_pairs={{0,16},{16,0},{1,17},{17,1},{2,18},{18,2},{3,19},{19,3},{4,20},{20... | collective-permute-start | bytes 393224 | tf_op jit(solution)/shard_map/while/body/eval_jaxpr/ppermute | solution.py:34
  343.3 0.5 copy-start.5
  377.8 5.1 %collective-permute-start.1 = (bf16[64,1024]{1,0:T(8,128)(2,1)S(1)}, bf16[64,1024]{1,0:T(8,128)(2,1)}, u32[]{:S(2)}, u32[]{:S(2)}) collective-permute-start(bf16[64,1024]{1,0:T(8,128)(2,1)S(1)} %get-tuple-element.675), channel_id=1, source_target_pairs={{0,16},{16,0},{1,17},{17,1},{2,18},{18,2},{3,19},{19,3},{4,20},{20... | collective-permute-start | bytes 393224 | tf_op jit(solution)/shard_map/while/body/eval_jaxpr/ppermute | solution.py:34
  389.6 0.5 copy-start.5
  424.0 5.1 %collective-permute-start.1 = (bf16[64,1024]{1,0:T(8,128)(2,1)S(1)}, bf16[64,1024]{1,0:T(8,128)(2,1)}, u32[]{:S(2)}, u32[]{:S(2)}) collective-permute-start(bf16[64,1024]{1,0:T(8,128)(2,1)S(1)} %get-tuple-element.675), channel_id=1, source_target_pairs={{0,16},{16,0},{1,17},{17,1},{2,18},{18,2},{3,19},{19,3},{4,20},{20... | collective-permute-start | bytes 393224 | tf_op jit(solution)/shard_map/while/body/eval_jaxpr/ppermute | solution.py:34
  438.3 30.8 %copy-start.2 = (bf16[2,64,1536]{2,1,0:T(8,128)(2,1)S(1)}, bf16[2,64,1536]{2,1,0:T(8,128)(2,1)}, u32[]{:S(2)}) copy-start(bf16[2,64,1536]{2,1,0:T(8,128)(2,1)} %param.21) | copy-start | bytes 1179652
  438.3 30.8 %copy-start.7 = (f32[2]{0:T(128)S(1)}, f32[2]{0:T(128)}, u32[]{:S(2)}) copy-start(f32[2]{0:T(128)} %copy-done.6) | copy-start | bytes 28
  469.1 9.3 %copy-start.9 = (f32[2]{0:T(128)S(1)}, f32[2]{0:T(128)}, u32[]{:S(2)}) copy-start(f32[2]{0:T(128)} %copy-done.8) | copy-start | bytes 28
Sparse Core Ops, SparseCore 0:
  127.7 29.8 all-reduce.17
  431.7 37.2 all-reduce.15
